TPU v7x, 32 devices: a whole 2x2x4 slice. The times are simulated.
32 devices in a mesh: groups: 2 (over y), state: 4 (over z), obs: 2 (over x), cores: 2 (over core).
Axes of the slice: x: 2, y: 2, z: 4, core: 2. Of those that a mesh axis runs over, the one named last changes fastest.
Arguments:
- ensemble: float32 [128, 128, 512], P(('groups', 'state'), ('obs', 'cores')), parts along dimension 0, may hold values from -6 to 6
- obs_value: float32 [2048], P('groups'), parts along dimension 0, may hold values from -8 to 8
- obs_var: float32 [2048], P('groups'), parts along dimension 0, may hold values from 0.25 to 4
- obs_cell: int32 [2048], P('groups'), parts along dimension 0, may hold values from 0 to 65535, as said below
- obs_order: int32 [2048], P('groups'), parts along dimension 0, may hold values from 0 to 1023, each once
- obs_blocks: int32 [2048, 6], P('groups'), parts along dimension 0, may hold values from 0 to 15, as said below
Outputs:
- posterior: float32 [128, 128, 512], P(('groups', 'state'), ('obs', 'cores')), parts along dimension 0
There are 2 independent parts, one for each index of `groups`. A program takes and returns all parts, laid end to end along the dimension named above; each array names one. Nothing has to cross between parts.
Inputs may be any that keep to these rules, and one draw needn't show every extreme that they name: `obs_cell`: each entry is the index row * 512 + column of a slab cell; observations gather around a few points of the slab. `obs_order`: every observation appears once. `obs_blocks`: row k holds 6 distinct blocks: first the block of observation k's cell, then the block in the same row band whose column band lies 4 // 2 bands away, then blocks whose row band and column band each differ from the first by at most one, cyclically.
All inputs are finite; a program needn't handle non-finite values.
Results may differ from a plain program's by a relative error of at most 0.0003.
Values sent between devices are 32-bit elements; how exact they have to be, the bound alone decides.
A program may use at most 64 MiB of HBM per device.

v0:
```python
import functools
import jax
import jax.numpy as jnp
from jax import lax
from jax.experimental import pallas as pl
from jax.experimental.pallas import tpu as pltpu
from jax.sharding import PartitionSpec as P

BATCHES = 4
BATCH_OBS = 256
CHUNKS = 4


def adjust_obs(prior_ens, obs_value, obs_var):
    members = prior_ens.shape[1]
    ens_mean = jnp.mean(prior_ens, axis=1)
    obs_anom = prior_ens - ens_mean[:, None]
    obs_spread = jnp.sum(obs_anom * obs_anom, axis=1) / (members - 1) + 1e-06
    post_var = 1.0 / (1.0 / obs_spread + 1.0 / obs_var)
    post_mean = post_var * (ens_mean / obs_spread + obs_value / obs_var)
    shrink = jnp.sqrt(post_var / obs_spread)
    obs_step = post_mean[:, None] + shrink[:, None] * obs_anom - prior_ens
    return (obs_anom, obs_step, obs_spread)


def distance_taper(obs_row, obs_col, cell_row, cell_col, rows_all, cols_all):
    row_gap = jnp.abs(cell_row[None, :] - obs_row[:, None])
    row_gap = jnp.minimum(row_gap, rows_all - row_gap)
    col_gap = jnp.abs(cell_col[None, :] - obs_col[:, None])
    col_gap = jnp.minimum(col_gap, cols_all - col_gap)
    row_term = (4.0 * row_gap.astype(jnp.float32) / rows_all) ** 2
    col_term = (4.0 * col_gap.astype(jnp.float32) / cols_all) ** 2
    return jnp.exp(-0.5 * (row_term + col_term))


def halves(x):
    high = x.astype(jnp.bfloat16)
    return high, (x - high.astype(jnp.float32)).astype(jnp.bfloat16)


def dot32(a, b):
    return jnp.dot(a, b, preferred_element_type=jnp.float32)


def gap_weight(a, b, extent):
    gap = jnp.abs(a - b)
    gap = jnp.minimum(gap, extent - gap)
    term = gap * (4.0 / extent)
    return jnp.exp(-0.5 * (term * term))


def split_anomaly(x):
    high, low = halves(x - jnp.mean(x, axis=0, keepdims=True))
    return jnp.concatenate([high, low, high], axis=0)


def kernel(n_state, n_cores, n_list, ens, lanes, subs, out, turned, fld, back, part, prior,
           anom3, step, row_w, col_w, pair_w, s1, r1, s2, r2, s3, r3, s_in, r_in, s_out, r_out):
    mem_dev, row_dev, cols_all = ens.shape
    bands = BATCHES
    rows_all = row_dev * bands
    col_dev = cols_all // n_state
    members = mem_dev * n_state
    z = lax.axis_index("state")
    band = lax.axis_index("obs") * n_cores + lax.axis_index("cores")
    rows_chunk = row_dev // CHUNKS
    f32 = jnp.float32

    def z_peer(i):
        return lax.rem(z + i, n_state)

    def band_peer(i):
        p = lax.rem(band + i, bands)
        return {"obs": p // n_cores, "cores": lax.rem(p, n_cores)}, p

    def remote(src, dst, send, recv, device):
        return pltpu.make_async_remote_copy(
            src_ref=src, dst_ref=dst, send_sem=send, recv_sem=recv,
            device_id=device, device_id_type=pl.DeviceIdType.MESH,
        )

    barrier = pltpu.get_barrier_semaphore()
    for i in range(1, n_state):
        pl.semaphore_signal(barrier, inc=1, device_id={"state": z_peer(i)}, device_id_type=pl.DeviceIdType.MESH)
    for i in range(1, bands):
        pl.semaphore_signal(barrier, inc=1, device_id=band_peer(i)[0], device_id_type=pl.DeviceIdType.MESH)

    flat = ens[...].reshape(mem_dev * row_dev, cols_all)
    high = flat.astype(jnp.bfloat16)
    rest = flat - high.astype(f32)
    mid = rest.astype(jnp.bfloat16)
    low = (rest - mid.astype(f32)).astype(jnp.bfloat16)
    col_iota = lax.broadcasted_iota(jnp.int32, (cols_all, BATCH_OBS), 0).astype(f32)
    row_iota = lax.broadcasted_iota(jnp.int32, (row_dev, BATCH_OBS), 0).astype(f32) + (band * row_dev).astype(f32)
    for b in range(BATCHES):
        o = pl.ds(b * BATCH_OBS, BATCH_OBS)
        onehot = jnp.where(col_iota == lanes[3:4, o], 1.0, 0.0).astype(jnp.bfloat16)
        picked = (dot32(low, onehot) + dot32(mid, onehot)) + dot32(high, onehot)
        mask = row_iota == lanes[2:3, o]
        picked = jnp.where(mask[None], picked.reshape(mem_dev, row_dev, BATCH_OBS), 0.0)
        turned_part = jnp.sum(picked, axis=1)
        part[bands + b] = turned_part

    pl.semaphore_wait(barrier, n_state - 1 + bands - 1)

    first = []
    for i in range(1, bands):
        device, p = band_peer(i)
        first.append(remote(part.at[bands + p], part.at[i], s1.at[i], r1.at[i], device))
        first[-1].start()
    for i in range(n_state):
        d = z_peer(i)
        piece = jnp.swapaxes(ens[:, :, pl.ds(pl.multiple_of(d * col_dev, col_dev), col_dev)], 0, 1)
        if i == 0:
            fld[:, pl.ds(pl.multiple_of(z * mem_dev, mem_dev), mem_dev), :] = piece
        else:
            turned[i] = piece
    for copy in first:
        copy.wait()
    mine = pl.ds(pl.multiple_of(z * mem_dev, mem_dev), mem_dev)
    total = part[bands + band]
    for i in range(1, bands):
        total = total + part[i]
    prior[band, mine, :] = total
    second = []
    for i in range(1, n_state):
        second.append(remote(prior.at[band, mine, :], prior.at[band, mine, :], s2.at[i], r2.at[i], {"state": z_peer(i)}))
        second[-1].start()
    inward = []
    for c in range(CHUNKS):
        rows = pl.ds(c * rows_chunk, rows_chunk)
        for i in range(1, n_state):
            inward.append(remote(turned.at[i, rows], fld.at[rows, mine, :], s_in.at[c, i], r_in.at[c, i], {"state": z_peer(i)}))
            inward[-1].start()

    my_block = (band * n_state + z).astype(f32)
    lane_cols = lax.broadcasted_iota(jnp.int32, (BATCH_OBS, col_dev), 1).astype(f32) + (z * col_dev).astype(f32)
    for b in range(BATCHES):
        o = pl.ds(b * BATCH_OBS, BATCH_OBS)
        row_w[b] = gap_weight(row_iota, lanes[2:3, o], rows_all)
        k_row, k_col = subs[o, 0:1], subs[o, 1:2]
        col_w[b] = gap_weight(lane_cols, k_col, cols_all)
        for later in range(b + 1, BATCHES):
            q = pl.ds(later * BATCH_OBS, BATCH_OBS)
            listed = subs[o, 2:3] == lanes[4:5, q]
            for l in range(1, n_list):
                listed = listed | (subs[o, 2 + l : 3 + l] == lanes[4:5, q])
            weight = gap_weight(k_row, lanes[2:3, q], rows_all) * gap_weight(k_col, lanes[3:4, q], cols_all)
            pair_w[b * BATCHES + later] = jnp.where(listed, weight, 0.0)

    for copy in second:
        copy.wait()
    third = []
    for i in range(1, bands):
        device, _ = band_peer(i)
        third.append(remote(prior.at[band], prior.at[band], s3.at[i], r3.at[i], device))
        third[-1].start()
    for copy in third:
        copy.wait()

    for b in range(BATCHES):
        o = pl.ds(b * BATCH_OBS, BATCH_OBS)
        x = prior[b]
        value, var = lanes[0:1, o], lanes[1:2, o]
        mean = jnp.mean(x, axis=0, keepdims=True)
        anom = x - mean
        spread = jnp.sum(anom * anom, axis=0, keepdims=True) / (members - 1) + 1e-06
        post_var = 1.0 / (1.0 / spread + 1.0 / var)
        post_mean = post_var * (mean / spread + value / var)
        shrink = jnp.sqrt(post_var / spread)
        scaled = (post_mean + shrink * anom - x) / ((members - 1) * spread)
        high, low = halves(anom)
        high = high.astype(f32)
        stacked = jnp.concatenate([high, high, low.astype(f32)], axis=0)
        left = stacked.T.astype(jnp.bfloat16)
        anom3[b] = left
        listed = lanes[5:6, o] == my_block
        for l in range(1, n_list):
            listed = listed | (lanes[5 + l : 6 + l, o] == my_block)
        step[b] = jnp.where(listed, scaled, 0.0)
        step_high, step_low = halves(scaled)
        both = jnp.concatenate([step_high, step_low], axis=0)
        for later in range(b + 1, BATCHES):
            y = prior[later]
            reg = dot32(left, split_anomaly(y)) * pair_w[b * BATCHES + later]
            reg_high, reg_low = halves(reg)
            big = dot32(both, reg_high)
            prior[later] = y + (big[:members] + (big[members:] + dot32(step_high, reg_low)))

    outward = []
    for c in range(CHUNKS):
        for copy in inward[c * (n_state - 1) : (c + 1) * (n_state - 1)]:
            copy.wait()

        def two_rows(p, carry, c=c):
            r = c * rows_chunk + 2 * p
            x = jnp.concatenate([fld[r], fld[r + 1]], axis=1)
            for b in range(BATCHES):
                cov = dot32(anom3[b], split_anomaly(x))
                adds = []
                for h in range(2):
                    reg = cov[:, h * col_dev : (h + 1) * col_dev] * col_w[b]
                    right = jnp.concatenate(halves(reg), axis=1)
                    left = jnp.concatenate(halves(step[b] * row_w[b, pl.ds(r + h, 1), :]), axis=0)
                    four = dot32(left, right)
                    adds.append(four[:members, :col_dev] + (four[:members, col_dev:] + four[members:, :col_dev]))
                x = x + jnp.concatenate(adds, axis=1)
            fld[r] = x[:, :col_dev]
            fld[r + 1] = x[:, col_dev:]
            return carry

        lax.fori_loop(0, rows_chunk // 2, two_rows, 0)
        rows = pl.ds(c * rows_chunk, rows_chunk)
        for i in range(1, n_state):
            d = z_peer(i)
            theirs = pl.ds(pl.multiple_of(d * mem_dev, mem_dev), mem_dev)
            outward.append(remote(fld.at[rows, theirs, :], back.at[i, rows], s_out.at[c, i], r_out.at[c, i], {"state": d}))
            outward[-1].start()
    out[:, :, pl.ds(pl.multiple_of(z * col_dev, col_dev), col_dev)] = jnp.swapaxes(fld[:, mine, :], 0, 1)
    for c in range(CHUNKS):
        rows = pl.ds(c * rows_chunk, rows_chunk)
        for i in range(1, n_state):
            outward[c * (n_state - 1) + i - 1].wait()
            s = lax.rem(z + n_state - i, n_state)
            out[:, rows, pl.ds(pl.multiple_of(s * col_dev, col_dev), col_dev)] = jnp.swapaxes(back[i, rows], 0, 1)


def fused(ensemble, value, var, obs_row, obs_col, obs_block, lists):
    n_state = lax.axis_size("state")
    n_cores = lax.axis_size("cores")
    mem_dev, row_dev, cols_all = ensemble.shape
    members = mem_dev * n_state
    col_dev = cols_all // n_state
    f32 = jnp.float32
    n_list = lists.shape[1]
    place = [obs_row.astype(f32), obs_col.astype(f32)]
    lanes = jnp.stack([value, var] + place + [obs_block.astype(f32)])
    lanes = jnp.concatenate([lanes, lists.astype(f32).T], axis=0)
    subs = jnp.concatenate([jnp.stack(place, axis=1), lists.astype(f32)], axis=1)
    vmem = pl.BlockSpec(memory_space=pltpu.VMEM)
    dma = pltpu.SemaphoreType.DMA
    return pl.pallas_call(
        functools.partial(kernel, n_state, n_cores, n_list),
        out_shape=jax.ShapeDtypeStruct(ensemble.shape, f32),
        in_specs=[vmem] * 3,
        out_specs=vmem,
        scratch_shapes=[
            pltpu.VMEM((n_state, row_dev, mem_dev, col_dev), f32),
            pltpu.VMEM((row_dev, members, col_dev), f32),
            pltpu.VMEM((n_state, row_dev, mem_dev, col_dev), f32),
            pltpu.VMEM((2 * BATCHES, mem_dev, BATCH_OBS), f32),
            pltpu.VMEM((BATCHES, members, BATCH_OBS), f32),
            pltpu.VMEM((BATCHES, BATCH_OBS, 3 * members), jnp.bfloat16),
            pltpu.VMEM((BATCHES, members, BATCH_OBS), f32),
            pltpu.VMEM((BATCHES, row_dev, BATCH_OBS), f32),
            pltpu.VMEM((BATCHES, BATCH_OBS, col_dev), f32),
            pltpu.VMEM((BATCHES * BATCHES, BATCH_OBS, BATCH_OBS), f32),
        ]
        + [dma((BATCHES,))] * 2
        + [dma((n_state,))] * 2
        + [dma((BATCHES,))] * 2
        + [dma((CHUNKS, n_state))] * 4,
        compiler_params=pltpu.CompilerParams(
            collective_id=0, has_side_effects=True, vmem_limit_bytes=40 * 2**20
        ),
    )(ensemble, lanes, subs)


def on_device(ensemble, obs_value, obs_var, obs_cell, obs_order, obs_blocks):
    n_state = lax.axis_size("state")
    n_obs = lax.axis_size("obs")
    n_cores = lax.axis_size("cores")
    mem_dev, row_dev, cols_all = ensemble.shape
    members = mem_dev * n_state
    col_dev = cols_all // n_state
    rows_all = row_dev * n_obs * n_cores
    row_band = lax.axis_index("obs") * n_cores + lax.axis_index("cores")
    row_start = row_band * row_dev
    col_start = lax.axis_index("state") * col_dev
    nobs = obs_order.shape[0]

    table = jnp.concatenate(
        [
            obs_value[:, None],
            obs_var[:, None],
            obs_cell.astype(jnp.float32)[:, None],
            obs_blocks.astype(jnp.float32),
        ],
        axis=1,
    )[obs_order]
    value, var = table[:, 0], table[:, 1]
    cells = table[:, 2].astype(jnp.int32)
    lists = table[:, 3:].astype(jnp.int32)
    obs_row = cells // cols_all
    obs_col = cells % cols_all
    obs_block = (obs_row // row_dev) * n_state + obs_col // col_dev

    if mem_dev % 8 == 0 and row_dev % CHUNKS == 0 and col_dev == 128 and n_obs * n_cores == BATCHES:
        return fused(ensemble, value, var, obs_row, obs_col, obs_block, lists)

    owned = (obs_row >= row_start) & (obs_row < row_start + row_dev)
    index = jnp.clip((obs_row - row_start) * cols_all + obs_col, 0, row_dev * cols_all - 1)
    mine = jnp.where(owned[None, :], ensemble.reshape(mem_dev, row_dev * cols_all)[:, index], 0.0)
    slot = jnp.zeros((members, nobs), jnp.float32)
    slot = lax.dynamic_update_slice_in_dim(slot, mine, lax.axis_index("state") * mem_dev, 0)
    at_obs = lax.psum(slot, ("state", "obs", "cores"))

    local_fields = lax.all_to_all(ensemble, "state", split_axis=2, concat_axis=0, tiled=True)
    count = row_dev * col_dev
    flat_index = jnp.arange(count, dtype=jnp.int32)
    cell_row = jnp.concatenate([row_start + flat_index // col_dev, obs_row])
    cell_col = jnp.concatenate([col_start + flat_index % col_dev, obs_col])
    my_block = row_band * n_state + lax.axis_index("state")
    cell_block = jnp.concatenate([jnp.full((count,), my_block, jnp.int32), obs_block])
    fields = jnp.concatenate([local_fields.reshape(members, count), at_obs], axis=1)
    for batch in range(BATCHES):
        part = slice(batch * BATCH_OBS, (batch + 1) * BATCH_OBS)
        prior_ens = fields[:, count + batch * BATCH_OBS : count + (batch + 1) * BATCH_OBS].T
        obs_anom, obs_step, obs_spread = adjust_obs(prior_ens, value[part], var[part])
        keep = count + nobs if batch < BATCHES - 1 else count
        listed = jnp.any(lists[part][:, :, None] == cell_block[None, None, :keep], axis=1)
        taper = distance_taper(
            obs_row[part], obs_col[part], cell_row[:keep], cell_col[:keep], rows_all, cols_all
        )
        taper_mask = jnp.where(listed, taper, 0.0)
        fields = fields[:, :keep]
        anomaly = fields - jnp.mean(fields, axis=0)
        covariance = jnp.dot(obs_anom, anomaly, precision=lax.Precision.HIGHEST) / (members - 1)
        regression = covariance * taper_mask / obs_spread[:, None]
        fields = fields + jnp.dot(obs_step.T, regression, precision=lax.Precision.HIGHEST)
    out_fields = fields.reshape(members, row_dev, col_dev)
    return lax.all_to_all(out_fields, "state", split_axis=0, concat_axis=2, tiled=True)


def solution(mesh):
    placed = (
        P(("groups", "state"), ("obs", "cores"), None),
        P("groups"),
        P("groups"),
        P("groups"),
        P("groups"),
        P("groups", None),
    )
    return jax.shard_map(
        on_device,
        mesh=mesh,
        in_specs=placed,
        out_specs=P(("groups", "state"), ("obs", "cores"), None),
        check_vma=False,
    )
```

profile of v0, /device:TPU:0, one launch (start us, length us, event | category | flops | bytes accessed | tf_op | source)
XLA Modules:
  0.0 65.0 jit_solution(14276218269343479503)
XLA Ops:
  0.0 0.0 copy-start.3
  0.0 0.7 %convert_element_type.72 = f32[1024]{0:T(1024)S(1)} convert(s32[1024]{0:T(1024)} %param.9) | non-fusion elementwise | flops 1024 | bytes 8192 | tf_op jit(solution)/shard_map/convert_element_type | solution.py:286
  0.7 0.0 copy-done.3
  0.7 0.0 copy-start.1
  0.7 0.0 copy-start.2
  0.7 0.8 %convert_element_type.73 = f32[1024,6]{0,1:T(8,128)S(1)} convert(s32[1024,6]{0,1:T(8,128)} %param.11) | non-fusion elementwise | flops 6144 | bytes 49152 | tf_op jit(solution)/shard_map/convert_element_type | solution.py:287
  1.5 0.0 copy-done.1
  1.5 0.0 copy-done.2
  1.6 0.2 copy.26
  1.8 2.8 %gather_fusion = f32[1024,9]{1,0:T(8,128)S(1)} fusion(f32[1024,9]{1,0:T(8,128)S(1)} %copy.26, s32[1024]{0:T(1024)S(1)} %fusion.7), kind=kCustom, calls=%fused_computation | custom fusion | bytes 77824 | tf_op jit(solution)/shard_map/gather | solution.py:282
  4.6 0.5 slice_reduce_fusion
  5.1 0.5 fusion
  5.6 0.5 fusion.1
  6.1 0.1 add_convert_fusion
  6.2 0.2 fusion.2
  6.4 0.0 copy-start
  6.4 0.3 pad_maximum_fusion.subs
  6.7 0.2 copy.27
  6.9 0.2 concatenate.10.lanes
  7.1 0.5 copy-done
  7.6 56.4 %shard_map.64 = f32[16,32,512]{2,1,0:T(8,128)S(1)} custom-call(f32[16,32,512]{2,1,0:T(8,128)S(1)} %copy-done, f32[11,1024]{1,0:T(8,128)S(1)} %concatenate.10.lanes, f32[1024,8]{1,0:T(8,128)S(1)} %pad_maximum_fusion.subs), custom_call_target="tpu_custom_call" | custom-call | tf_op jit(solution)/shard_map/pallas_call | solution.py:242
  64.0 1.0 %copy.29 = f32[16,32,512]{2,1,0:T(8,128)} copy(f32[16,32,512]{2,1,0:T(8,128)S(1)} %shard_map.64) | data formatting | bytes 2097152
  (4 shorter events, 0.1 us)
Async XLA Ops:
  0.0 0.7 %copy-start.3 = (s32[1024]{0:T(1024)S(1)}, s32[1024]{0:T(1024)}, u32[]{:S(2)}) copy-start(s32[1024]{0:T(1024)} %param.10) | copy-start | bytes 12292
  0.7 0.8 %copy-start.1 = (f32[1024]{0:T(1024)S(1)}, f32[1024]{0:T(1024)}, u32[]{:S(2)}) copy-start(f32[1024]{0:T(1024)} %param.8) | copy-start | bytes 12292
  0.7 0.8 %copy-start.2 = (f32[1024]{0:T(1024)S(1)}, f32[1024]{0:T(1024)}, u32[]{:S(2)}) copy-start(f32[1024]{0:T(1024)} %param.7) | copy-start | bytes 12292
  6.4 1.2 %copy-start = (f32[16,32,512]{2,1,0:T(8,128)S(1)}, f32[16,32,512]{2,1,0:T(8,128)}, u32[]{:S(2)}) copy-start(f32[16,32,512]{2,1,0:T(8,128)} %ens.1) | copy-start | bytes 3145732
where the time goes:
time: 65.2 us; the launch traced here: 65 us
  Pallas kernels  56.4 us (87%)
  local copies, waits for them, and re-layouts  5.38 us (8%)
  other arithmetic  3.1 us (5%)
    pallas_call x1, Pallas kernels, fused(): pl.pallas_call(functools.partial(kernel, n_state, n_cores, n_list), out_s...  56.4 us
    gather x1, local copies, waits for them, and re-layouts, on_device(): jnp.concatenate([obs_value[:, None], obs_var[:, None], obs_cell.astype(jn...  2.81 us
    unnamed x9, local copies, waits for them, and re-layouts  1.51 us

commit v1 on v0

--- a/solution.py
+++ b/solution.py
@@ -38,6 +38,13 @@
     return high, (x - high.astype(jnp.float32)).astype(jnp.bfloat16)
 
 
+def thirds(x):
+    high = x.astype(jnp.bfloat16)
+    rest = x - high.astype(jnp.float32)
+    mid = rest.astype(jnp.bfloat16)
+    return high, mid, (rest - mid.astype(jnp.float32)).astype(jnp.bfloat16)
+
+
 def dot32(a, b):
     return jnp.dot(a, b, preferred_element_type=jnp.float32)
 
@@ -54,7 +61,7 @@
     return jnp.concatenate([high, low, high], axis=0)
 
 
-def kernel(n_state, n_cores, n_list, ens, lanes, subs, out, turned, fld, back, part, prior,
+def kernel(n_state, n_cores, n_list, ens, table, order, out, lanes, subs, turned, fld, back, part, prior,
            anom3, step, row_w, col_w, pair_w, s1, r1, s2, r2, s3, r3, s_in, r_in, s_out, r_out):
     mem_dev, row_dev, cols_all = ens.shape
     bands = BATCHES
@@ -85,11 +92,38 @@
     for i in range(1, bands):
         pl.semaphore_signal(barrier, inc=1, device_id=band_peer(i)[0], device_id_type=pl.DeviceIdType.MESH)
 
+    mine = pl.ds(pl.multiple_of(z * mem_dev, mem_dev), mem_dev)
+    for i in range(n_state):
+        d = z_peer(i)
+        piece = jnp.swapaxes(ens[:, :, pl.ds(pl.multiple_of(d * col_dev, col_dev), col_dev)], 0, 1)
+        if i == 0:
+            fld[:, mine, :] = piece
+        else:
+            turned[i] = piece
+    pl.semaphore_wait(barrier, n_state - 1 + bands - 1)
+    inward = []
+
+    def send_in(c):
+        rows = pl.ds(c * rows_chunk, rows_chunk)
+        for i in range(1, n_state):
+            inward.append(remote(turned.at[i, rows], fld.at[rows, mine, :], s_in.at[c, i], r_in.at[c, i], {"state": z_peer(i)}))
+            inward[-1].start()
+
+    send_in(0)
+
+    flat_table = jnp.concatenate(thirds(table[...]), axis=0)
+    obs_iota = lax.broadcasted_iota(jnp.int32, (table.shape[1], BATCH_OBS), 0)
+    height = table.shape[0]
+    for b in range(BATCHES):
+        o = pl.ds(b * BATCH_OBS, BATCH_OBS)
+        onehot = jnp.where(obs_iota == order[0:1, o], 1.0, 0.0).astype(jnp.bfloat16)
+        picked = dot32(flat_table, onehot)
+        ordered = (picked[2 * height :] + picked[height : 2 * height]) + picked[:height]
+        lanes[:, o] = ordered
+        subs[o, :] = ordered.T
+
     flat = ens[...].reshape(mem_dev * row_dev, cols_all)
-    high = flat.astype(jnp.bfloat16)
-    rest = flat - high.astype(f32)
-    mid = rest.astype(jnp.bfloat16)
-    low = (rest - mid.astype(f32)).astype(jnp.bfloat16)
+    high, mid, low = thirds(flat)
     col_iota = lax.broadcasted_iota(jnp.int32, (cols_all, BATCH_OBS), 0).astype(f32)
     row_iota = lax.broadcasted_iota(jnp.int32, (row_dev, BATCH_OBS), 0).astype(f32) + (band * row_dev).astype(f32)
     for b in range(BATCHES):
@@ -98,26 +132,15 @@
         picked = (dot32(low, onehot) + dot32(mid, onehot)) + dot32(high, onehot)
         mask = row_iota == lanes[2:3, o]
         picked = jnp.where(mask[None], picked.reshape(mem_dev, row_dev, BATCH_OBS), 0.0)
-        turned_part = jnp.sum(picked, axis=1)
-        part[bands + b] = turned_part
-
-    pl.semaphore_wait(barrier, n_state - 1 + bands - 1)
+        part[bands + b] = jnp.sum(picked, axis=1)
 
     first = []
     for i in range(1, bands):
         device, p = band_peer(i)
         first.append(remote(part.at[bands + p], part.at[i], s1.at[i], r1.at[i], device))
         first[-1].start()
-    for i in range(n_state):
-        d = z_peer(i)
-        piece = jnp.swapaxes(ens[:, :, pl.ds(pl.multiple_of(d * col_dev, col_dev), col_dev)], 0, 1)
-        if i == 0:
-            fld[:, pl.ds(pl.multiple_of(z * mem_dev, mem_dev), mem_dev), :] = piece
-        else:
-            turned[i] = piece
     for copy in first:
         copy.wait()
-    mine = pl.ds(pl.multiple_of(z * mem_dev, mem_dev), mem_dev)
     total = part[bands + band]
     for i in range(1, bands):
         total = total + part[i]
@@ -126,25 +149,21 @@
     for i in range(1, n_state):
         second.append(remote(prior.at[band, mine, :], prior.at[band, mine, :], s2.at[i], r2.at[i], {"state": z_peer(i)}))
         second[-1].start()
-    inward = []
-    for c in range(CHUNKS):
-        rows = pl.ds(c * rows_chunk, rows_chunk)
-        for i in range(1, n_state):
-            inward.append(remote(turned.at[i, rows], fld.at[rows, mine, :], s_in.at[c, i], r_in.at[c, i], {"state": z_peer(i)}))
-            inward[-1].start()
+    for c in range(1, CHUNKS):
+        send_in(c)
 
     my_block = (band * n_state + z).astype(f32)
     lane_cols = lax.broadcasted_iota(jnp.int32, (BATCH_OBS, col_dev), 1).astype(f32) + (z * col_dev).astype(f32)
     for b in range(BATCHES):
         o = pl.ds(b * BATCH_OBS, BATCH_OBS)
         row_w[b] = gap_weight(row_iota, lanes[2:3, o], rows_all)
-        k_row, k_col = subs[o, 0:1], subs[o, 1:2]
+        k_row, k_col = subs[o, 2:3], subs[o, 3:4]
         col_w[b] = gap_weight(lane_cols, k_col, cols_all)
         for later in range(b + 1, BATCHES):
             q = pl.ds(later * BATCH_OBS, BATCH_OBS)
-            listed = subs[o, 2:3] == lanes[4:5, q]
+            listed = subs[o, 5:6] == lanes[4:5, q]
             for l in range(1, n_list):
-                listed = listed | (subs[o, 2 + l : 3 + l] == lanes[4:5, q])
+                listed = listed | (subs[o, 5 + l : 6 + l] == lanes[4:5, q])
             weight = gap_weight(k_row, lanes[2:3, q], rows_all) * gap_weight(k_col, lanes[3:4, q], cols_all)
             pair_w[b * BATCHES + later] = jnp.where(listed, weight, 0.0)
 
@@ -225,18 +244,20 @@
             out[:, rows, pl.ds(pl.multiple_of(s * col_dev, col_dev), col_dev)] = jnp.swapaxes(back[i, rows], 0, 1)
 
 
-def fused(ensemble, value, var, obs_row, obs_col, obs_block, lists):
+def fused(ensemble, obs_value, obs_var, obs_cell, obs_order, obs_blocks):
     n_state = lax.axis_size("state")
     n_cores = lax.axis_size("cores")
     mem_dev, row_dev, cols_all = ensemble.shape
     members = mem_dev * n_state
     col_dev = cols_all // n_state
     f32 = jnp.float32
-    n_list = lists.shape[1]
-    place = [obs_row.astype(f32), obs_col.astype(f32)]
-    lanes = jnp.stack([value, var] + place + [obs_block.astype(f32)])
-    lanes = jnp.concatenate([lanes, lists.astype(f32).T], axis=0)
-    subs = jnp.concatenate([jnp.stack(place, axis=1), lists.astype(f32)], axis=1)
+    nobs, n_list = obs_blocks.shape
+    height = -(-(5 + n_list) // 16) * 16
+    row, col = obs_cell // cols_all, obs_cell % cols_all
+    block = (row // row_dev) * n_state + col // col_dev
+    table = jnp.stack([obs_value, obs_var, row.astype(f32), col.astype(f32), block.astype(f32)])
+    spare = jnp.zeros((height - 5 - n_list, nobs), f32)
+    table = jnp.concatenate([table, obs_blocks.astype(f32).T, spare], axis=0)
     vmem = pl.BlockSpec(memory_space=pltpu.VMEM)
     dma = pltpu.SemaphoreType.DMA
     return pl.pallas_call(
@@ -245,6 +266,8 @@
         in_specs=[vmem] * 3,
         out_specs=vmem,
         scratch_shapes=[
+            pltpu.VMEM((height, nobs), f32),
+            pltpu.VMEM((nobs, height), f32),
             pltpu.VMEM((n_state, row_dev, mem_dev, col_dev), f32),
             pltpu.VMEM((row_dev, members, col_dev), f32),
             pltpu.VMEM((n_state, row_dev, mem_dev, col_dev), f32),
@@ -263,7 +286,7 @@
         compiler_params=pltpu.CompilerParams(
             collective_id=0, has_side_effects=True, vmem_limit_bytes=40 * 2**20
         ),
-    )(ensemble, lanes, subs)
+    )(ensemble, table, obs_order.reshape(1, nobs))
 
 
 def on_device(ensemble, obs_value, obs_var, obs_cell, obs_order, obs_blocks):
@@ -278,6 +301,9 @@
     row_start = row_band * row_dev
     col_start = lax.axis_index("state") * col_dev
     nobs = obs_order.shape[0]
+
+    if mem_dev % 16 == 0 and row_dev % (2 * CHUNKS) == 0 and col_dev == 128 and n_obs * n_cores == BATCHES:
+        return fused(ensemble, obs_value, obs_var, obs_cell, obs_order, obs_blocks)
 
     table = jnp.concatenate(
         [
@@ -294,9 +320,6 @@
     obs_row = cells // cols_all
     obs_col = cells % cols_all
     obs_block = (obs_row // row_dev) * n_state + obs_col // col_dev
-
-    if mem_dev % 8 == 0 and row_dev % CHUNKS == 0 and col_dev == 128 and n_obs * n_cores == BATCHES:
-        return fused(ensemble, value, var, obs_row, obs_col, obs_block, lists)
 
     owned = (obs_row >= row_start) & (obs_row < row_start + row_dev)
     index = jnp.clip((obs_row - row_start) * cols_all + obs_col, 0, row_dev * cols_all - 1)

time: 65.2 us -> 58.6 us (0.90); the launches traced: 65 us -> 57.6 us
  Pallas kernels: 56.4 us -> 53.2 us
  other arithmetic: 3.1 us -> 0.72 us
  local copies, waits for them, and re-layouts: 5.38 us -> 3.63 us
    pallas_call x1, Pallas kernels: 56.4 us -> 53.2 us  [fused(): pl.pallas_call(functools.partial(kernel, n_state, n_cores, n_list), out_s...]
    gather x1 -> x0, local copies, waits for them, and re-layouts: 2.81 us -> none  [on_device(): jnp.concatenate([obs_value[:, None], obs_var[:, None], obs_cell.astype(jn...]
    convert_element_type x8 -> x1, other arithmetic: 2.72 us -> 0.71 us  [fused(): block.astype(f32)]
    unnamed x9 -> x11, local copies, waits for them, and re-layouts: 1.51 us -> 3.47 us
where the time goes in v1:
time: 58.6 us; the launch traced here: 57.6 us
  Pallas kernels  53.2 us (91%)
  local copies, waits for them, and re-layouts  3.63 us (6%)
  other arithmetic  0.72 us (1%)
    pallas_call x1, Pallas kernels, fused(): pl.pallas_call(functools.partial(kernel, n_state, n_cores, n_list), out_s...  53.2 us
    unnamed x11, local copies, waits for them, and re-layouts  3.47 us

profile of v1, /device:TPU:0, one launch (start us, length us, event | category | flops | bytes accessed | tf_op | source)
XLA Modules:
  0.0 57.6 jit_solution(16931330532835288349)
XLA Ops:
  0.0 0.0 copy-start.2
  0.0 0.7 %fusion.3 = (f32[1024]{0:T(1024)S(1)}, f32[1024]{0:T(1024)S(1)}, f32[1024]{0:T(1024)S(1)}) fusion(s32[1024]{0:T(1024)} %param.9), kind=kLoop, calls=%fused_computation.17 | loop fusion | flops 55296 | bytes 16384 | tf_op jit(solution)/shard_map/convert_element_type | solution.py:258
  0.7 0.1 copy-done.2
  0.8 0.0 copy-start.3
  0.8 0.0 copy-start.4
  0.8 0.7 %copy-done.3 = f32[1024]{0:T(1024)S(1)} copy-done((f32[1024]{0:T(1024)S(1)}, f32[1024]{0:T(1024)}, u32[]{:S(2)}) %copy-start.3) | copy-done | bytes 4120
  1.5 0.0 copy-done.4
  1.5 0.0 copy-start.1
  1.5 0.2 concatenate.3.table
  1.6 0.5 copy-done.1
  2.2 0.0 copy-start
  2.2 1.2 %copy-done = f32[16,32,512]{2,1,0:T(8,128)S(1)} copy-done((f32[16,32,512]{2,1,0:T(8,128)S(1)}, f32[16,32,512]{2,1,0:T(8,128)}, u32[]{:S(2)}) %copy-start) | copy-done | bytes 1048600
  3.4 53.2 %shard_map.64 = f32[16,32,512]{2,1,0:T(8,128)S(1)} custom-call(f32[16,32,512]{2,1,0:T(8,128)S(1)} %copy-done, f32[16,1024]{1,0:T(8,128)S(1)} %concatenate.3.table, s32[1,1024]{1,0:T(1,128)S(1)} %bitcast.8), custom_call_target="tpu_custom_call" | custom-call | tf_op jit(solution)/shard_map/pallas_call | solution.py:263
  56.6 1.0 %copy.8 = f32[16,32,512]{2,1,0:T(8,128)} copy(f32[16,32,512]{2,1,0:T(8,128)S(1)} %shard_map.64) | data formatting | bytes 2097152
  (2 shorter events, 0.0 us)
Async XLA Ops:
  0.0 0.8 %copy-start.2 = (s32[1024,6]{0,1:T(8,128)S(1)}, s32[1024,6]{0,1:T(8,128)}, u32[]{:S(2)}) copy-start(s32[1024,6]{0,1:T(8,128)} %param.11) | copy-start | bytes 73732
  0.8 0.7 %copy-start.3 = (f32[1024]{0:T(1024)S(1)}, f32[1024]{0:T(1024)}, u32[]{:S(2)}) copy-start(f32[1024]{0:T(1024)} %param.7) | copy-start | bytes 12292
  0.8 0.7 %copy-start.4 = (f32[1024]{0:T(1024)S(1)}, f32[1024]{0:T(1024)}, u32[]{:S(2)}) copy-start(f32[1024]{0:T(1024)} %param.8) | copy-start | bytes 12292
  1.5 0.7 %copy-start.1 = (s32[1024]{0:T(1024)S(1)}, s32[1024]{0:T(1024)}, u32[]{:S(2)}) copy-start(s32[1024]{0:T(1024)} %param.10) | copy-start | bytes 12292
  2.2 1.2 %copy-start = (f32[16,32,512]{2,1,0:T(8,128)S(1)}, f32[16,32,512]{2,1,0:T(8,128)}, u32[]{:S(2)}) copy-start(f32[16,32,512]{2,1,0:T(8,128)} %ens.1) | copy-start | bytes 3145732

commit v2 on v1

--- a/solution.py
+++ b/solution.py
@@ -9,6 +9,7 @@
 BATCHES = 4
 BATCH_OBS = 256
 CHUNKS = 4
+PAIRS = 2
 
 
 def adjust_obs(prior_ens, obs_value, obs_var):
@@ -110,6 +111,7 @@
             inward[-1].start()
 
     send_in(0)
+    send_in(1)
 
     flat_table = jnp.concatenate(thirds(table[...]), axis=0)
     obs_iota = lax.broadcasted_iota(jnp.int32, (table.shape[1], BATCH_OBS), 0)
@@ -149,7 +151,7 @@
     for i in range(1, n_state):
         second.append(remote(prior.at[band, mine, :], prior.at[band, mine, :], s2.at[i], r2.at[i], {"state": z_peer(i)}))
         second[-1].start()
-    for c in range(1, CHUNKS):
+    for c in range(2, CHUNKS):
         send_in(c)
 
     my_block = (band * n_state + z).astype(f32)
@@ -211,24 +213,27 @@
         for copy in inward[c * (n_state - 1) : (c + 1) * (n_state - 1)]:
             copy.wait()
 
-        def two_rows(p, carry, c=c):
-            r = c * rows_chunk + 2 * p
-            x = jnp.concatenate([fld[r], fld[r + 1]], axis=1)
+        def some_rows(p, carry, c=c):
+            start = c * rows_chunk + 2 * PAIRS * p
+            xs = [jnp.concatenate([fld[start + 2 * n], fld[start + 2 * n + 1]], axis=1) for n in range(PAIRS)]
             for b in range(BATCHES):
-                cov = dot32(anom3[b], split_anomaly(x))
-                adds = []
-                for h in range(2):
-                    reg = cov[:, h * col_dev : (h + 1) * col_dev] * col_w[b]
-                    right = jnp.concatenate(halves(reg), axis=1)
-                    left = jnp.concatenate(halves(step[b] * row_w[b, pl.ds(r + h, 1), :]), axis=0)
-                    four = dot32(left, right)
-                    adds.append(four[:members, :col_dev] + (four[:members, col_dev:] + four[members:, :col_dev]))
-                x = x + jnp.concatenate(adds, axis=1)
-            fld[r] = x[:, :col_dev]
-            fld[r + 1] = x[:, col_dev:]
+                covs = [dot32(anom3[b], split_anomaly(x)) for x in xs]
+                for n in range(PAIRS):
+                    adds = []
+                    for h in range(2):
+                        row = start + 2 * n + h
+                        reg = covs[n][:, h * col_dev : (h + 1) * col_dev] * col_w[b]
+                        right = jnp.concatenate(halves(reg), axis=1)
+                        left = jnp.concatenate(halves(step[b] * row_w[b, pl.ds(row, 1), :]), axis=0)
+                        four = dot32(left, right)
+                        adds.append(four[:members, :col_dev] + (four[:members, col_dev:] + four[members:, :col_dev]))
+                    xs[n] = xs[n] + jnp.concatenate(adds, axis=1)
+            for n in range(PAIRS):
+                fld[start + 2 * n] = xs[n][:, :col_dev]
+                fld[start + 2 * n + 1] = xs[n][:, col_dev:]
             return carry
 
-        lax.fori_loop(0, rows_chunk // 2, two_rows, 0)
+        lax.fori_loop(0, rows_chunk // (2 * PAIRS), some_rows, 0)
         rows = pl.ds(c * rows_chunk, rows_chunk)
         for i in range(1, n_state):
             d = z_peer(i)
@@ -302,7 +307,7 @@
     col_start = lax.axis_index("state") * col_dev
     nobs = obs_order.shape[0]
 
-    if mem_dev % 16 == 0 and row_dev % (2 * CHUNKS) == 0 and col_dev == 128 and n_obs * n_cores == BATCHES:
+    if mem_dev % 16 == 0 and row_dev % (2 * PAIRS * CHUNKS) == 0 and col_dev == 128 and n_obs * n_cores == BATCHES:
         return fused(ensemble, obs_value, obs_var, obs_cell, obs_order, obs_blocks)
 
     table = jnp.concatenate(

time: 58.6 us -> 63.7 us (1.087); the launches traced: 57.6 us -> 63.4 us
  Pallas kernels: 53.2 us -> 59 us
    pallas_call x1, Pallas kernels: 53.2 us -> 59 us  [fused(): pl.pallas_call(functools.partial(kernel, n_state, n_cores, n_list), out_s...]
where the time goes in v2:
time: 63.7 us; the launch traced here: 63.4 us
  Pallas kernels  59 us (93%)
  local copies, waits for them, and re-layouts  3.63 us (6%)
  other arithmetic  0.72 us (1%)
    pallas_call x1, Pallas kernels, fused(): pl.pallas_call(functools.partial(kernel, n_state, n_cores, n_list), out_s...  59 us
    unnamed x11, local copies, waits for them, and re-layouts  3.47 us

profile of v2, /device:TPU:0, one launch (start us, length us, event | category | flops | bytes accessed | tf_op | source)
XLA Modules:
  0.0 63.4 jit_solution(12778132599027422845)
XLA Ops:
  0.0 0.0 copy-start.2
  0.0 0.7 %fusion.3 = (f32[1024]{0:T(1024)S(1)}, f32[1024]{0:T(1024)S(1)}, f32[1024]{0:T(1024)S(1)}) fusion(s32[1024]{0:T(1024)} %param.9), kind=kLoop, calls=%fused_computation.17 | loop fusion | flops 55296 | bytes 16384 | tf_op jit(solution)/shard_map/convert_element_type | solution.py:263
  0.7 0.1 copy-done.2
  0.8 0.0 copy-start.3
  0.8 0.0 copy-start.4
  0.8 0.7 %copy-done.3 = f32[1024]{0:T(1024)S(1)} copy-done((f32[1024]{0:T(1024)S(1)}, f32[1024]{0:T(1024)}, u32[]{:S(2)}) %copy-start.3) | copy-done | bytes 4120
  1.5 0.0 copy-done.4
  1.5 0.0 copy-start.1
  1.5 0.2 concatenate.3.table
  1.6 0.5 copy-done.1
  2.2 0.0 copy-start
  2.2 1.2 %copy-done = f32[16,32,512]{2,1,0:T(8,128)S(1)} copy-done((f32[16,32,512]{2,1,0:T(8,128)S(1)}, f32[16,32,512]{2,1,0:T(8,128)}, u32[]{:S(2)}) %copy-start) | copy-done | bytes 1048600
  3.4 59.0 %shard_map.64 = f32[16,32,512]{2,1,0:T(8,128)S(1)} custom-call(f32[16,32,512]{2,1,0:T(8,128)S(1)} %copy-done, f32[16,1024]{1,0:T(8,128)S(1)} %concatenate.3.table, s32[1,1024]{1,0:T(1,128)S(1)} %bitcast.8), custom_call_target="tpu_custom_call" | custom-call | tf_op jit(solution)/shard_map/pallas_call | solution.py:268
  62.4 1.0 %copy.8 = f32[16,32,512]{2,1,0:T(8,128)} copy(f32[16,32,512]{2,1,0:T(8,128)S(1)} %shard_map.64) | data formatting | bytes 2097152
  (2 shorter events, 0.0 us)
Async XLA Ops:
  0.0 0.8 %copy-start.2 = (s32[1024,6]{0,1:T(8,128)S(1)}, s32[1024,6]{0,1:T(8,128)}, u32[]{:S(2)}) copy-start(s32[1024,6]{0,1:T(8,128)} %param.11) | copy-start | bytes 73732
  0.8 0.7 %copy-start.3 = (f32[1024]{0:T(1024)S(1)}, f32[1024]{0:T(1024)}, u32[]{:S(2)}) copy-start(f32[1024]{0:T(1024)} %param.7) | copy-start | bytes 12292
  0.8 0.7 %copy-start.4 = (f32[1024]{0:T(1024)S(1)}, f32[1024]{0:T(1024)}, u32[]{:S(2)}) copy-start(f32[1024]{0:T(1024)} %param.8) | copy-start | bytes 12292
  1.5 0.7 %copy-start.1 = (s32[1024]{0:T(1024)S(1)}, s32[1024]{0:T(1024)}, u32[]{:S(2)}) copy-start(s32[1024]{0:T(1024)} %param.10) | copy-start | bytes 12292
  2.2 1.2 %copy-start = (f32[16,32,512]{2,1,0:T(8,128)S(1)}, f32[16,32,512]{2,1,0:T(8,128)}, u32[]{:S(2)}) copy-start(f32[16,32,512]{2,1,0:T(8,128)} %ens.1) | copy-start | bytes 3145732

commit v3 on v2

--- a/solution.py
+++ b/solution.py
@@ -8,7 +8,7 @@
 
 BATCHES = 4
 BATCH_OBS = 256
-CHUNKS = 4
+CHUNKS = 8
 PAIRS = 2
 
 
@@ -241,10 +241,11 @@
             outward.append(remote(fld.at[rows, theirs, :], back.at[i, rows], s_out.at[c, i], r_out.at[c, i], {"state": d}))
             outward[-1].start()
     out[:, :, pl.ds(pl.multiple_of(z * col_dev, col_dev), col_dev)] = jnp.swapaxes(fld[:, mine, :], 0, 1)
-    for c in range(CHUNKS):
-        rows = pl.ds(c * rows_chunk, rows_chunk)
+    for c in range(0, CHUNKS, 2):
+        rows = pl.ds(c * rows_chunk, 2 * rows_chunk)
         for i in range(1, n_state):
             outward[c * (n_state - 1) + i - 1].wait()
+            outward[(c + 1) * (n_state - 1) + i - 1].wait()
             s = lax.rem(z + n_state - i, n_state)
             out[:, rows, pl.ds(pl.multiple_of(s * col_dev, col_dev), col_dev)] = jnp.swapaxes(back[i, rows], 0, 1)
 

time: 63.7 us -> 58.4 us (0.917)
  Pallas kernels: 59 us -> 53.7 us
    pallas_call x1, Pallas kernels: 59 us -> 53.7 us  [fused(): pl.pallas_call(functools.partial(kernel, n_state, n_cores, n_list), out_s...]
where the time goes in v3:
time: 58.4 us; the launch traced here: 58.1 us
  Pallas kernels  53.7 us (92%)
  local copies, waits for them, and re-layouts  3.63 us (6%)
  other arithmetic  0.72 us (1%)
    pallas_call x1, Pallas kernels, fused(): pl.pallas_call(functools.partial(kernel, n_state, n_cores, n_list), out_s...  53.7 us
    unnamed x11, local copies, waits for them, and re-layouts  3.47 us

profile of v3, /device:TPU:0, one launch (start us, length us, event | category | flops | bytes accessed | tf_op | source)
XLA Modules:
  0.0 58.1 jit_solution(17388094208017502625)
XLA Ops:
  0.0 0.0 copy-start.2
  0.0 0.7 %fusion.3 = (f32[1024]{0:T(1024)S(1)}, f32[1024]{0:T(1024)S(1)}, f32[1024]{0:T(1024)S(1)}) fusion(s32[1024]{0:T(1024)} %param.9), kind=kLoop, calls=%fused_computation.17 | loop fusion | flops 55296 | bytes 16384 | tf_op jit(solution)/shard_map/convert_element_type | solution.py:264
  0.7 0.1 copy-done.2
  0.8 0.0 copy-start.3
  0.8 0.0 copy-start.4
  0.8 0.7 %copy-done.3 = f32[1024]{0:T(1024)S(1)} copy-done((f32[1024]{0:T(1024)S(1)}, f32[1024]{0:T(1024)}, u32[]{:S(2)}) %copy-start.3) | copy-done | bytes 4120
  1.5 0.0 copy-done.4
  1.5 0.0 copy-start.1
  1.5 0.2 concatenate.3.table
  1.6 0.5 copy-done.1
  2.2 0.0 copy-start
  2.2 1.2 %copy-done = f32[16,32,512]{2,1,0:T(8,128)S(1)} copy-done((f32[16,32,512]{2,1,0:T(8,128)S(1)}, f32[16,32,512]{2,1,0:T(8,128)}, u32[]{:S(2)}) %copy-start) | copy-done | bytes 1048600
  3.4 53.7 %shard_map.64 = f32[16,32,512]{2,1,0:T(8,128)S(1)} custom-call(f32[16,32,512]{2,1,0:T(8,128)S(1)} %copy-done, f32[16,1024]{1,0:T(8,128)S(1)} %concatenate.3.table, s32[1,1024]{1,0:T(1,128)S(1)} %bitcast.8), custom_call_target="tpu_custom_call" | custom-call | tf_op jit(solution)/shard_map/pallas_call | solution.py:269
  57.1 1.0 %copy.8 = f32[16,32,512]{2,1,0:T(8,128)} copy(f32[16,32,512]{2,1,0:T(8,128)S(1)} %shard_map.64) | data formatting | bytes 2097152
  (2 shorter events, 0.0 us)
Async XLA Ops:
  0.0 0.8 %copy-start.2 = (s32[1024,6]{0,1:T(8,128)S(1)}, s32[1024,6]{0,1:T(8,128)}, u32[]{:S(2)}) copy-start(s32[1024,6]{0,1:T(8,128)} %param.11) | copy-start | bytes 73732
  0.8 0.7 %copy-start.3 = (f32[1024]{0:T(1024)S(1)}, f32[1024]{0:T(1024)}, u32[]{:S(2)}) copy-start(f32[1024]{0:T(1024)} %param.7) | copy-start | bytes 12292
  0.8 0.7 %copy-start.4 = (f32[1024]{0:T(1024)S(1)}, f32[1024]{0:T(1024)}, u32[]{:S(2)}) copy-start(f32[1024]{0:T(1024)} %param.8) | copy-start | bytes 12292
  1.5 0.7 %copy-start.1 = (s32[1024]{0:T(1024)S(1)}, s32[1024]{0:T(1024)}, u32[]{:S(2)}) copy-start(s32[1024]{0:T(1024)} %param.10) | copy-start | bytes 12292
  2.2 1.2 %copy-start = (f32[16,32,512]{2,1,0:T(8,128)S(1)}, f32[16,32,512]{2,1,0:T(8,128)}, u32[]{:S(2)}) copy-start(f32[16,32,512]{2,1,0:T(8,128)} %ens.1) | copy-start | bytes 3145732

commit v4 on v3

--- a/solution.py
+++ b/solution.py
@@ -111,7 +111,6 @@
             inward[-1].start()
 
     send_in(0)
-    send_in(1)
 
     flat_table = jnp.concatenate(thirds(table[...]), axis=0)
     obs_iota = lax.broadcasted_iota(jnp.int32, (table.shape[1], BATCH_OBS), 0)
@@ -151,7 +150,7 @@
     for i in range(1, n_state):
         second.append(remote(prior.at[band, mine, :], prior.at[band, mine, :], s2.at[i], r2.at[i], {"state": z_peer(i)}))
         second[-1].start()
-    for c in range(2, CHUNKS):
+    for c in range(1, CHUNKS):
         send_in(c)
 
     my_block = (band * n_state + z).astype(f32)

time: 58.4 us -> 61.2 us (1.048)
  Pallas kernels: 53.7 us -> 56.5 us
    pallas_call x1, Pallas kernels: 53.7 us -> 56.5 us  [fused(): pl.pallas_call(functools.partial(kernel, n_state, n_cores, n_list), out_s...]
where the time goes in v4:
time: 61.2 us; the launch traced here: 60.9 us
  Pallas kernels  56.5 us (92%)
  local copies, waits for them, and re-layouts  3.63 us (6%)
  other arithmetic  0.72 us (1%)
    pallas_call x1, Pallas kernels, fused(): pl.pallas_call(functools.partial(kernel, n_state, n_cores, n_list), out_s...  56.5 us
    unnamed x11, local copies, waits for them, and re-layouts  3.47 us

profile of v4, /device:TPU:0, one launch (start us, length us, event | category | flops | bytes accessed | tf_op | source)
XLA Modules:
  0.0 60.9 jit_solution(12748288828239548371)
XLA Ops:
  0.0 0.0 copy-start.2
  0.0 0.7 %fusion.3 = (f32[1024]{0:T(1024)S(1)}, f32[1024]{0:T(1024)S(1)}, f32[1024]{0:T(1024)S(1)}) fusion(s32[1024]{0:T(1024)} %param.9), kind=kLoop, calls=%fused_computation.17 | loop fusion | flops 55296 | bytes 16384 | tf_op jit(solution)/shard_map/convert_element_type | solution.py:263
  0.7 0.1 copy-done.2
  0.8 0.0 copy-start.3
  0.8 0.0 copy-start.4
  0.8 0.7 %copy-done.3 = f32[1024]{0:T(1024)S(1)} copy-done((f32[1024]{0:T(1024)S(1)}, f32[1024]{0:T(1024)}, u32[]{:S(2)}) %copy-start.3) | copy-done | bytes 4120
  1.5 0.0 copy-done.4
  1.5 0.0 copy-start.1
  1.5 0.2 concatenate.3.table
  1.6 0.5 copy-done.1
  2.2 0.0 copy-start
  2.2 1.2 %copy-done = f32[16,32,512]{2,1,0:T(8,128)S(1)} copy-done((f32[16,32,512]{2,1,0:T(8,128)S(1)}, f32[16,32,512]{2,1,0:T(8,128)}, u32[]{:S(2)}) %copy-start) | copy-done | bytes 1048600
  3.4 56.5 %shard_map.64 = f32[16,32,512]{2,1,0:T(8,128)S(1)} custom-call(f32[16,32,512]{2,1,0:T(8,128)S(1)} %copy-done, f32[16,1024]{1,0:T(8,128)S(1)} %concatenate.3.table, s32[1,1024]{1,0:T(1,128)S(1)} %bitcast.8), custom_call_target="tpu_custom_call" | custom-call | tf_op jit(solution)/shard_map/pallas_call | solution.py:268
  59.9 1.0 %copy.8 = f32[16,32,512]{2,1,0:T(8,128)} copy(f32[16,32,512]{2,1,0:T(8,128)S(1)} %shard_map.64) | data formatting | bytes 2097152
  (2 shorter events, 0.0 us)
Async XLA Ops:
  0.0 0.8 %copy-start.2 = (s32[1024,6]{0,1:T(8,128)S(1)}, s32[1024,6]{0,1:T(8,128)}, u32[]{:S(2)}) copy-start(s32[1024,6]{0,1:T(8,128)} %param.11) | copy-start | bytes 73732
  0.8 0.7 %copy-start.3 = (f32[1024]{0:T(1024)S(1)}, f32[1024]{0:T(1024)}, u32[]{:S(2)}) copy-start(f32[1024]{0:T(1024)} %param.7) | copy-start | bytes 12292
  0.8 0.7 %copy-start.4 = (f32[1024]{0:T(1024)S(1)}, f32[1024]{0:T(1024)}, u32[]{:S(2)}) copy-start(f32[1024]{0:T(1024)} %param.8) | copy-start | bytes 12292
  1.5 0.7 %copy-start.1 = (s32[1024]{0:T(1024)S(1)}, s32[1024]{0:T(1024)}, u32[]{:S(2)}) copy-start(s32[1024]{0:T(1024)} %param.10) | copy-start | bytes 12292
  2.2 1.2 %copy-start = (f32[16,32,512]{2,1,0:T(8,128)S(1)}, f32[16,32,512]{2,1,0:T(8,128)}, u32[]{:S(2)}) copy-start(f32[16,32,512]{2,1,0:T(8,128)} %ens.1) | copy-start | bytes 3145732
